TPU v7x, 512 devices: a whole 4x8x8 slice. The times are simulated.
512 devices in a mesh: space: 16 (over z, core), member: 8 (over y), tm: 4 (over x).
Axes of the slice: x: 4, y: 8, z: 8, core: 2. Of those that a mesh axis runs over, the one named last changes fastest.
Arguments:
- ens_pert: bfloat16 [8, 128, 131072], P('tm', 'member', 'space'), may hold values from -6 to 6
- weights: float32 [128, 512], P('member', 'space'), may hold values from -6 to 6
- foot_block: int32 [8, 16, 16, 8, 32], P('tm', 'space'), may hold values from 0 to 31
- foot_offset: int32 [8, 16, 16, 8, 32], P('tm', 'space'), may hold values from 0 to 255
- innovation: float32 [8, 16, 8, 16, 32], P('tm', 'space', 'member'), may hold values from -6 to 6
- inv_var: float32 [8, 16, 8, 16, 32], P('tm', 'space', 'member'), may hold values from 0.25 to 2.5
- obs_count: int32 [8, 16, 8, 16], P('tm', 'space', 'member'), may hold values from 1 to 32, as said below
Outputs:
- gradient: float32 [128, 512], P('member', 'space')
Inputs may be any that keep to these rules, and one draw needn't show every extreme that they name: `obs_count`: live slots come first among the 32 slots; in every time slot one destination tile has all 32 slots live from every owner.
All inputs are finite; a program needn't handle non-finite values.
Results may differ from a plain program's by a relative error of at most 0.0029.
Values sent between devices are 32-bit elements; how exact they have to be, the bound alone decides.
No kernel may reach another device: no remote copies, remote signals or barrier semaphores. Data moves between devices by JAX's collectives and lax.ppermute only.
A program may use at most 64 MiB of HBM per device.

v0:
```python
import math
import jax
import jax.numpy as jnp
from jax import lax
from jax.sharding import PartitionSpec as P

BLOCK = 256


def split_pair(values, axis_at):
    upper = lax.optimization_barrier(values.astype(jnp.bfloat16))
    lower = (values - upper.astype(jnp.float32)).astype(jnp.bfloat16)
    return jnp.concatenate([upper, lower], axis=axis_at)


def shards(ens_pert, weights, foot_block, foot_offset, innovation, inv_var, obs_count):
    tile_count = lax.axis_size("space")
    group_count = lax.axis_size("member")
    slot_count, members, cell_dev = ens_pert.shape
    capacity = foot_block.shape[-1]
    blk_dev = cell_dev // BLOCK
    norm_scale = 1.0 / math.sqrt(members * group_count - 1)
    pert_blocks = ens_pert.reshape(slot_count, members, blk_dev, BLOCK)
    weights_rounded = weights.astype(jnp.bfloat16)
    partial_field = norm_scale * jnp.einsum(
        "tmbc,mb->tbc", pert_blocks, weights_rounded, preferred_element_type=jnp.float32
    )
    split_field = split_pair(partial_field, 1)
    block_rows = jnp.transpose(foot_block.reshape(slot_count, tile_count, -1), (1, 0, 2))
    offset_rows = jnp.transpose(foot_offset.reshape(slot_count, tile_count, -1), (1, 0, 2))
    block_iota = lax.broadcasted_iota(jnp.int32, (1, blk_dev, 1), 1)
    offset_iota = lax.broadcasted_iota(jnp.int32, (1, 1, BLOCK), 2)

    def pick_tile(pair):
        blk_ids, off_ids = pair
        off_hot = (off_ids[:, :, None] == offset_iota).astype(jnp.bfloat16)
        proj = jnp.einsum("tjc,tkc->tjk", split_field, off_hot, preferred_element_type=jnp.float32)
        value = proj[:, :blk_dev] + proj[:, blk_dev:]
        chosen = jnp.where(blk_ids[:, None, :] == block_iota, value, jnp.zeros_like(value))
        return jnp.sum(chosen, axis=1)

    picked = jnp.transpose(lax.map(pick_tile, (block_rows, offset_rows)), (1, 0, 2))
    arrived_vals = lax.all_to_all(
        picked.reshape(slot_count, tile_count * group_count, capacity),
        ("space", "member"),
        split_axis=1,
        concat_axis=1,
        tiled=True,
    )
    model_obs = jnp.sum(arrived_vals.reshape(slot_count, tile_count, group_count, capacity), axis=2)
    innov_local = innovation.reshape(slot_count, tile_count, capacity)
    obs_weight = inv_var.reshape(slot_count, tile_count, capacity)
    counts = obs_count.reshape(slot_count, tile_count, 1)
    is_live = lax.broadcasted_iota(jnp.int32, (slot_count, tile_count, capacity), 2) < counts
    residual = jnp.where(
        is_live, obs_weight * (model_obs - innov_local), jnp.zeros_like(innov_local)
    )
    residual = residual.reshape(slot_count, 1, 1, tile_count, capacity)
    spread = lax.all_gather(residual, "member", axis=2, tiled=True)
    arrived = lax.all_to_all(spread, "space", split_axis=3, concat_axis=1, tiled=True)
    arrived_rows = jnp.transpose(arrived.reshape(slot_count, tile_count, -1), (1, 0, 2))

    def add_tile(total, triple):
        blk_ids, off_ids, values = triple
        off_hot = (off_ids[:, :, None] == offset_iota).astype(jnp.bfloat16)
        placed = jnp.where(
            blk_ids[:, None, :] == block_iota, values[:, None, :], jnp.zeros((), jnp.float32)
        )
        both = split_pair(placed, 1)
        part_sum = jnp.einsum("tjk,tkc->tjc", both, off_hot, preferred_element_type=jnp.float32)
        return (total + (part_sum[:, :blk_dev] + part_sum[:, blk_dev:]), None)

    start_total = jnp.zeros((slot_count, blk_dev, BLOCK), jnp.float32)
    adjoint, _ = lax.scan(add_tile, start_total, (block_rows, offset_rows, arrived_rows))
    adjoint_rounded = adjoint.astype(jnp.bfloat16)
    local_grad = jnp.einsum(
        "tmbc,tbc->mb", pert_blocks, adjoint_rounded, preferred_element_type=jnp.float32
    )
    summed = lax.psum(local_grad, "tm")
    return weights + norm_scale * summed


def solution(mesh):
    in_specs = (
        P("tm", "member", "space"),
        P("member", "space"),
        P("tm", "space", None, None, None),
        P("tm", "space", None, None, None),
        P("tm", "space", "member", None, None),
        P("tm", "space", "member", None, None),
        P("tm", "space", "member", None),
    )
    out_specs = P("member", "space")
    return jax.shard_map(shards, mesh=mesh, in_specs=in_specs, out_specs=out_specs, check_vma=False)
```

profile of v0, /device:TPU:1, one launch (start us, length us, event | category | flops | bytes accessed | tf_op | source)
XLA Modules:
  0.0 95.3 jit_solution(16273810836954491873)
XLA Ops:
  0.0 0.7 convert_bitcast_fusion.1
  0.8 1.2 %fusion.21 = f32[32,1,2,256]{3,1,2,0:T(1,128)S(1)} fusion(bf16[16,32,1,1]{0,2,3,1:T(2,128)(2,1)S(1)} %copy.38, bf16[2,2,32,8,256]{4,3,2,1,0:T(8,128)(2,1)} %bitcast.84), kind=kOutput, calls=%fused_computation.32 | convolution fusion | flops 524288 | bytes 590848 | tf_op jit(solution)/shard_map/tmbc,mb->tbc/dot_general | solution.py:25
  2.1 0.8 copy-done.1
  3.2 5.8 %while.22 = (s32[]{:T(128)}, f32[16,2,256]{2,1,0:T(2,128)S(1)}, s32[16,2,256]{2,1,0:T(2,128)S(1)}, s32[16,2,256]{2,1,0:T(2,128)S(1)}, bf16[2,64,256]{2,1,0:T(8,128)(2,1)S(1)}, /*index=5*/s32[]{:T(128)}) while((s32[]{:T(128)}, f32[16,2,256]{2,1,0:T(2,128)S(1)}, s32[16,2,256]{2,1,0:T(2,128)S(1)}, s32[16,2,256]{2,1,0:T(2,128)S(1)}, ...), condition=%wide.region_2.3_spmd.clone, body=%wide.region_0.2_spmd.clone.sunk | while | flops 16973312 | bytes 346189 | solution.py:42
  9.1 0.8 copy.33
  9.9 18.4 %all-to-all-start = ((f32[2,128,32]{2,0,1:T(2,128)}), f32[2,128,32]{2,0,1:T(2,128)S(1)}, u32[]{:S(2)}, u32[]{:S(2)}) async-start(f32[2,128,32]{2,0,1:T(2,128)} %copy.33), calls=%async_computation | async-start | bytes 262144 | tf_op jit(solution)/shard_map/all_to_all | solution.py:43
  28.3 0.7 copy-done.6
  29.1 11.8 %all-to-all-done = f32[2,128,32]{2,0,1:T(2,128)S(1)} async-done(((f32[2,128,32]{2,0,1:T(2,128)}), f32[2,128,32]{2,0,1:T(2,128)S(1)}, u32[]{:S(2)}, u32[]{:S(2)}) %all-to-all-start) | async-done | bytes 32800 | tf_op jit(solution)/shard_map/all_to_all | solution.py:43
  41.0 18.2 %all_gather.3 = f32[2,1,8,16,32]{4,3,1,0,2:T(8,128)S(1)} all-gather(f32[2,1,1,16,32]{4,3,1,0,2:T(8,128)S(1)} %copy.36), channel_id=1, replica_groups=mesh['space'=16,'member'=8,'tm'=4] {'member'}, dimensions={2}, use_global_device_ids=true | all-gather | bytes 36864 | tf_op jit(solution)/shard_map/all_gather | solution.py:59
  59.4 0.7 reshape.54
  60.1 10.0 %all-to-all-start.1 = ((f32[16,1,512]{2,1,0:T(1,128)}), f32[16,1,512]{2,1,0:T(1,128)S(1)}, u32[]{:S(2)}, u32[]{:S(2)}) async-start(f32[16,1,512]{2,1,0:T(1,128)} %reshape.54), calls=%async_computation.1 | async-start | bytes 65536 | tf_op jit(solution)/shard_map/all_to_all | solution.py:60
  70.1 7.5 %all-to-all-done.1 = f32[16,1,512]{2,1,0:T(1,128)S(1)} async-done(((f32[16,1,512]{2,1,0:T(1,128)}), f32[16,1,512]{2,1,0:T(1,128)S(1)}, u32[]{:S(2)}, u32[]{:S(2)}) %all-to-all-start.1) | async-done | bytes 32800 | tf_op jit(solution)/shard_map/all_to_all | solution.py:60
  77.6 0.5 broadcast.27
  78.1 0.7 reduce
  79.0 6.6 %while.23 = (s32[]{:T(128)}, f32[2,32,256]{2,1,0:T(8,128)S(1)}, s32[16,2,256]{2,1,0:T(2,128)S(1)}, f32[16,2,256]{2,1,0:T(2,128)S(1)}, s32[16,2,256]{2,1,0:T(2,128)S(1)}, /*index=5*/s32[]{:T(128)}, s32[]{:T(128)}) while((s32[]{:T(128)}, f32[2,32,256]{2,1,0:T(8,128)S(1)}, s32[16,2,256]{2,1,0:T(2,128)S(1)}, ...), condition=%wide.region_5.6_spmd.clone, body=%wide.region_4.5_spmd.clone.sunk | while | flops 17203200 | bytes 579679 | solution.py:74
  79.1 0.3 fusion.40
  80.0 0.3 fusion.40
  80.4 0.3 fusion.40
  80.8 0.3 fusion.40
  81.2 0.3 fusion.40
  81.6 0.3 fusion.40
  82.0 0.3 fusion.40
  82.4 0.3 fusion.40
  82.8 0.3 fusion.40
  83.2 0.3 fusion.40
  83.7 0.3 fusion.40
  84.1 0.3 fusion.40
  84.5 0.3 fusion.40
  84.9 0.3 fusion.40
  85.3 0.3 fusion.40
  86.0 8.7 %psum.7 = f32[16,32]{1,0:T(8,128)S(1)} all-reduce(f32[16,32]{1,0:T(8,128)S(1)} %bitcast.88), channel_id=1, replica_groups=mesh['space'=16,'member'=8,'tm'=4] {'tm'}, use_global_device_ids=true, to_apply=%region_6.7 | all-reduce | flops 512 | bytes 4096 | tf_op jit(solution)/shard_map/psum | solution.py:79
  94.7 0.6 multiply_add_fusion
  (179 shorter events, 8.0 us)
Async XLA Ops:
  2.1 0.9 copy-start.1
  2.1 1.0 %copy-start.2 = (s32[2,1,16,8,32]{4,3,2,1,0:T(8,128)S(1)}, s32[2,1,16,8,32]{4,3,2,1,0:T(8,128)}, u32[]{:S(2)}) copy-start(s32[2,1,16,8,32]{4,3,2,1,0:T(8,128)} %param.14) | copy-start | bytes 98308
  9.9 31.0 %all-to-all-start = ((f32[2,128,32]{2,0,1:T(2,128)}), f32[2,128,32]{2,0,1:T(2,128)S(1)}, u32[]{:S(2)}, u32[]{:S(2)}) async-start(f32[2,128,32]{2,0,1:T(2,128)} %copy.33), calls=%async_computation | async-start | bytes 262144 | tf_op jit(solution)/shard_map/all_to_all | solution.py:43
  28.3 0.7 copy-start.6
  29.1 11.8 %copy-start.4 = (f32[2,1,1,16,32]{4,3,2,1,0:T(8,128)S(1)}, f32[2,1,1,16,32]{4,3,2,1,0:T(8,128)}, u32[]{:S(2)}) copy-start(f32[2,1,1,16,32]{4,3,2,1,0:T(8,128)} %param.16) | copy-start | bytes 12292
  29.1 11.8 %copy-start.5 = (f32[2,1,1,16,32]{4,3,2,1,0:T(8,128)S(1)}, f32[2,1,1,16,32]{4,3,2,1,0:T(8,128)}, u32[]{:S(2)}) copy-start(f32[2,1,1,16,32]{4,3,2,1,0:T(8,128)} %param.15) | copy-start | bytes 12292
  60.1 17.5 %all-to-all-start.1 = ((f32[16,1,512]{2,1,0:T(1,128)}), f32[16,1,512]{2,1,0:T(1,128)S(1)}, u32[]{:S(2)}, u32[]{:S(2)}) async-start(f32[16,1,512]{2,1,0:T(1,128)} %reshape.54), calls=%async_computation.1 | async-start | bytes 65536 | tf_op jit(solution)/shard_map/all_to_all | solution.py:60
  79.0 6.6 %copy-start = (bf16[2,16,8192]{2,1,0:T(8,128)(2,1)S(1)}, bf16[2,16,8192]{2,1,0:T(8,128)(2,1)}, u32[]{:S(2)}) copy-start(bf16[2,16,8192]{2,1,0:T(8,128)(2,1)} %param.11) | copy-start | bytes 1572868
  86.0 8.7 %copy-start.3 = (f32[16,32]{1,0:T(8,128)S(1)}, f32[16,32]{1,0:T(8,128)}, u32[]{:S(2)}) copy-start(f32[16,32]{1,0:T(8,128)} %param.12) | copy-start | bytes 6148
where the time goes:
time: 95.7 us; the launch traced here: 95.3 us
  starting transfers between devices  28.4 us (30%)
  blocking collectives  26.9 us (28%)
  waiting for transfers between devices  19.2 us (20%)
  matrix products  10.3 us (11%)
  local copies, waits for them, and re-layouts  5.06 us (5%)
  other arithmetic  3.52 us (4%)
  loops' own time  1.59 us (2%)
    all_to_all x1, starting transfers between devices, shards(): lax.all_to_all(picked.reshape(slot_count, tile_count * group_count, capac...  18.4 us
    all_gather x1, blocking collectives, shards(): spread = lax.all_gather(residual, 'member', axis=2, tiled=True)  18.2 us
    all_to_all x1, waiting for transfers between devices, shards(): lax.all_to_all(picked.reshape(slot_count, tile_count * group_count, capac...  11.8 us
    all_to_all x1, starting transfers between devices, shards(): lax.all_to_all(spread, 'space', split_axis=3, concat_axis=1, tiled=True)  10 us
    psum x1, blocking collectives, shards(): summed = lax.psum(local_grad, 'tm')  8.7 us
    all_to_all x1, waiting for transfers between devices, shards(): lax.all_to_all(spread, 'space', split_axis=3, concat_axis=1, tiled=True)  7.48 us
    dot_general x16, matrix products, add_tile(): jnp.einsum('tjk,tkc->tjc', both, off_hot, preferred_element_type=jnp.floa...  4.45 us
    dot_general x16, matrix products, pick_tile(): jnp.einsum('tjc,tkc->tjk', split_field, off_hot, preferred_element_type=j...  4.35 us
  transfers between devices with their start and end apart: 2, of which 2 were waited for; matrix products, arithmetic and copies ran while one was open for 0% of the time, Pallas kernels for 0%

commit v1 on v0

--- a/solution.py
+++ b/solution.py
@@ -5,6 +5,14 @@
 from jax.sharding import PartitionSpec as P
 
 BLOCK = 256
+
+
+def doubling_sum(shard, axis):
+    size, acc = (lax.axis_size(axis), shard)
+    for far in [1 << k for k in range(size.bit_length() - 1)]:
+        swap = [(i, i ^ far) for i in range(size)]
+        acc = acc + lax.ppermute(acc, axis, swap)
+    return acc
 
 
 def split_pair(values, axis_at):
@@ -76,7 +84,7 @@
     local_grad = jnp.einsum(
         "tmbc,tbc->mb", pert_blocks, adjoint_rounded, preferred_element_type=jnp.float32
     )
-    summed = lax.psum(local_grad, "tm")
+    summed = doubling_sum(local_grad, "tm")
     return weights + norm_scale * summed
 
 

time: 95.7 us -> 98.7 us (1.031); the launches traced: 95.3 us -> 97.1 us
  blocking collectives: 26.9 us -> 18.2 us
  starting transfers between devices: 28.4 us -> 36.3 us
  waiting for transfers between devices: 19.2 us -> 21.8 us
    psum x1 -> x0, blocking collectives: 8.7 us -> none  [shards(): summed = lax.psum(local_grad, 'tm')]
    ppermute x0 -> x2, starting transfers between devices: none -> 7.9 us  [doubling_sum(): acc = acc + lax.ppermute(acc, axis, swap)]
    ppermute x0 -> x2, waiting for transfers between devices: none -> 2.51 us  [doubling_sum(): acc = acc + lax.ppermute(acc, axis, swap)]
  transfers between devices with their start and end apart: 2 -> 4, of which waited for: 2 -> 4; matrix products, arithmetic and copies ran while one was open for 0% -> 0% of each run, Pallas kernels for 0% -> 0%
where the time goes in v1:
time: 98.7 us; the launch traced here: 97.1 us
  starting transfers between devices  36.3 us (37%)
  waiting for transfers between devices  21.8 us (22%)
  blocking collectives  18.2 us (18%)
  matrix products  10.3 us (10%)
  local copies, waits for them, and re-layouts  5.1 us (5%)
  other arithmetic  3.53 us (4%)
  loops' own time  1.59 us (2%)
    all_to_all x1, starting transfers between devices, shards(): lax.all_to_all(picked.reshape(slot_count, tile_count * group_count, capac...  18.4 us
    all_gather x1, blocking collectives, shards(): spread = lax.all_gather(residual, 'member', axis=2, tiled=True)  18.2 us
    all_to_all x1, waiting for transfers between devices, shards(): lax.all_to_all(picked.reshape(slot_count, tile_count * group_count, capac...  11.8 us
    all_to_all x1, starting transfers between devices, shards(): lax.all_to_all(spread, 'space', split_axis=3, concat_axis=1, tiled=True)  10 us
    ppermute x2, starting transfers between devices, doubling_sum(): acc = acc + lax.ppermute(acc, axis, swap)  7.9 us
    all_to_all x1, waiting for transfers between devices, shards(): lax.all_to_all(spread, 'space', split_axis=3, concat_axis=1, tiled=True)  7.48 us
    dot_general x16, matrix products, add_tile(): jnp.einsum('tjk,tkc->tjc', both, off_hot, preferred_element_type=jnp.floa...  4.45 us
    dot_general x16, matrix products, pick_tile(): jnp.einsum('tjc,tkc->tjk', split_field, off_hot, preferred_element_type=j...  4.35 us
  transfers between devices with their start and end apart: 4, of which 4 were waited for; matrix products, arithmetic and copies ran while one was open for 0% of the time, Pallas kernels for 0%

profile of v1, /device:TPU:1, one launch (start us, length us, event | category | flops | bytes accessed | tf_op | source)
XLA Modules:
  0.0 97.1 jit_solution(11555246383229461473)
XLA Ops:
  0.0 0.7 convert_bitcast_fusion.1
  0.8 1.2 %fusion.21 = f32[32,1,2,256]{3,1,2,0:T(1,128)S(1)} fusion(bf16[16,32,1,1]{0,2,3,1:T(2,128)(2,1)S(1)} %copy.38, bf16[2,2,32,8,256]{4,3,2,1,0:T(8,128)(2,1)} %bitcast.85), kind=kOutput, calls=%fused_computation.32 | convolution fusion | flops 524288 | bytes 590848 | tf_op jit(solution)/shard_map/tmbc,mb->tbc/dot_general | solution.py:33
  2.1 0.8 copy-done.1
  3.2 5.8 %while.22 = (s32[]{:T(128)}, f32[16,2,256]{2,1,0:T(2,128)S(1)}, s32[16,2,256]{2,1,0:T(2,128)S(1)}, s32[16,2,256]{2,1,0:T(2,128)S(1)}, bf16[2,64,256]{2,1,0:T(8,128)(2,1)S(1)}, /*index=5*/s32[]{:T(128)}) while((s32[]{:T(128)}, f32[16,2,256]{2,1,0:T(2,128)S(1)}, s32[16,2,256]{2,1,0:T(2,128)S(1)}, s32[16,2,256]{2,1,0:T(2,128)S(1)}, ...), condition=%wide.region_2.3_spmd.clone, body=%wide.region_0.2_spmd.clone.sunk | while | flops 16973312 | bytes 346189 | solution.py:50
  9.1 0.8 copy.33
  9.9 18.4 %all-to-all-start = ((f32[2,128,32]{2,0,1:T(2,128)}), f32[2,128,32]{2,0,1:T(2,128)S(1)}, u32[]{:S(2)}, u32[]{:S(2)}) async-start(f32[2,128,32]{2,0,1:T(2,128)} %copy.33), calls=%async_computation | async-start | bytes 262144 | tf_op jit(solution)/shard_map/all_to_all | solution.py:51
  28.3 0.7 copy-done.6
  29.1 11.8 %all-to-all-done = f32[2,128,32]{2,0,1:T(2,128)S(1)} async-done(((f32[2,128,32]{2,0,1:T(2,128)}), f32[2,128,32]{2,0,1:T(2,128)S(1)}, u32[]{:S(2)}, u32[]{:S(2)}) %all-to-all-start) | async-done | bytes 32800 | tf_op jit(solution)/shard_map/all_to_all | solution.py:51
  41.0 18.2 %all_gather.3 = f32[2,1,8,16,32]{4,3,1,0,2:T(8,128)S(1)} all-gather(f32[2,1,1,16,32]{4,3,1,0,2:T(8,128)S(1)} %copy.36), channel_id=1, replica_groups=mesh['space'=16,'member'=8,'tm'=4] {'member'}, dimensions={2}, use_global_device_ids=true | all-gather | bytes 36864 | tf_op jit(solution)/shard_map/all_gather | solution.py:67
  59.4 0.7 reshape.54
  60.1 10.0 %all-to-all-start.1 = ((f32[16,1,512]{2,1,0:T(1,128)}), f32[16,1,512]{2,1,0:T(1,128)S(1)}, u32[]{:S(2)}, u32[]{:S(2)}) async-start(f32[16,1,512]{2,1,0:T(1,128)} %reshape.54), calls=%async_computation.1 | async-start | bytes 65536 | tf_op jit(solution)/shard_map/all_to_all | solution.py:68
  70.1 7.5 %all-to-all-done.1 = f32[16,1,512]{2,1,0:T(1,128)S(1)} async-done(((f32[16,1,512]{2,1,0:T(1,128)}), f32[16,1,512]{2,1,0:T(1,128)S(1)}, u32[]{:S(2)}, u32[]{:S(2)}) %all-to-all-start.1) | async-done | bytes 32800 | tf_op jit(solution)/shard_map/all_to_all | solution.py:68
  77.6 0.6 broadcast.27
  78.1 0.7 reduce
  79.1 6.6 %while.23 = (s32[]{:T(128)}, f32[2,32,256]{2,1,0:T(8,128)S(1)}, s32[16,2,256]{2,1,0:T(2,128)S(1)}, f32[16,2,256]{2,1,0:T(2,128)S(1)}, s32[16,2,256]{2,1,0:T(2,128)S(1)}, /*index=5*/s32[]{:T(128)}, s32[]{:T(128)}) while((s32[]{:T(128)}, f32[2,32,256]{2,1,0:T(8,128)S(1)}, s32[16,2,256]{2,1,0:T(2,128)S(1)}, ...), condition=%wide.region_5.6_spmd.clone, body=%wide.region_4.5_spmd.clone.sunk | while | flops 17203200 | bytes 579679 | solution.py:82
  79.6 0.3 fusion.40
  80.0 0.3 fusion.40
  80.4 0.3 fusion.40
  80.8 0.3 fusion.40
  81.2 0.3 fusion.40
  81.6 0.3 fusion.40
  82.0 0.3 fusion.40
  82.5 0.3 fusion.40
  82.9 0.3 fusion.40
  83.3 0.3 fusion.40
  83.7 0.3 fusion.40
  84.1 0.3 fusion.40
  86.0 3.3 %collective-permute-start = (f32[16,32]{1,0:T(8,128)S(1)}, f32[16,32]{1,0:T(8,128)S(1)}, u32[]{:S(2)}, u32[]{:S(2)}) collective-permute-start(f32[16,32]{1,0:T(8,128)S(1)} %bitcast.89), channel_id=1, source_target_pairs={{0,1},{1,0},{2,3},{3,2},{4,5},{5,4},{6,7},{7,6},{8,9},{9,8},{10,11... | collective-permute-start | bytes 6152 | tf_op jit(solution)/shard_map/ppermute | solution.py:14
  89.3 1.3 %collective-permute-done = f32[16,32]{1,0:T(8,128)S(1)} collective-permute-done((f32[16,32]{1,0:T(8,128)S(1)}, f32[16,32]{1,0:T(8,128)S(1)}, u32[]{:S(2)}, u32[]{:S(2)}) %collective-permute-start) | collective-permute-done | bytes 2080 | tf_op jit(solution)/shard_map/ppermute | solution.py:14
  90.6 4.6 %collective-permute-start.1 = (f32[16,32]{1,0:T(8,128)S(1)}, f32[16,32]{1,0:T(8,128)S(1)}, u32[]{:S(2)}, u32[]{:S(2)}) collective-permute-start(f32[16,32]{1,0:T(8,128)S(1)} %bitcast_add_fusion), channel_id=1, source_target_pairs={{0,2},{1,3},{2,0},{3,1},{4,6},{5,7},{6,4},{7,5},{8,10},{9,11},{10,... | collective-permute-start | bytes 6152 | tf_op jit(solution)/shard_map/ppermute | solution.py:14
  95.2 1.2 %collective-permute-done.1 = f32[16,32]{1,0:T(8,128)S(1)} collective-permute-done((f32[16,32]{1,0:T(8,128)S(1)}, f32[16,32]{1,0:T(8,128)S(1)}, u32[]{:S(2)}, u32[]{:S(2)}) %collective-permute-start.1) | collective-permute-done | bytes 2080 | tf_op jit(solution)/shard_map/ppermute | solution.py:14
  96.5 0.6 multiply_add_fusion
  (183 shorter events, 8.8 us)
Async XLA Ops:
  2.1 0.9 copy-start.1
  2.1 1.0 %copy-start.2 = (s32[2,1,16,8,32]{4,3,2,1,0:T(8,128)S(1)}, s32[2,1,16,8,32]{4,3,2,1,0:T(8,128)}, u32[]{:S(2)}) copy-start(s32[2,1,16,8,32]{4,3,2,1,0:T(8,128)} %param.14) | copy-start | bytes 98308
  9.9 31.0 %all-to-all-start = ((f32[2,128,32]{2,0,1:T(2,128)}), f32[2,128,32]{2,0,1:T(2,128)S(1)}, u32[]{:S(2)}, u32[]{:S(2)}) async-start(f32[2,128,32]{2,0,1:T(2,128)} %copy.33), calls=%async_computation | async-start | bytes 262144 | tf_op jit(solution)/shard_map/all_to_all | solution.py:51
  28.3 0.7 copy-start.6
  29.1 11.8 %copy-start.4 = (f32[2,1,1,16,32]{4,3,2,1,0:T(8,128)S(1)}, f32[2,1,1,16,32]{4,3,2,1,0:T(8,128)}, u32[]{:S(2)}) copy-start(f32[2,1,1,16,32]{4,3,2,1,0:T(8,128)} %param.16) | copy-start | bytes 12292
  29.1 11.8 %copy-start.5 = (f32[2,1,1,16,32]{4,3,2,1,0:T(8,128)S(1)}, f32[2,1,1,16,32]{4,3,2,1,0:T(8,128)}, u32[]{:S(2)}) copy-start(f32[2,1,1,16,32]{4,3,2,1,0:T(8,128)} %param.15) | copy-start | bytes 12292
  60.1 17.5 %all-to-all-start.1 = ((f32[16,1,512]{2,1,0:T(1,128)}), f32[16,1,512]{2,1,0:T(1,128)S(1)}, u32[]{:S(2)}, u32[]{:S(2)}) async-start(f32[16,1,512]{2,1,0:T(1,128)} %reshape.54), calls=%async_computation.1 | async-start | bytes 65536 | tf_op jit(solution)/shard_map/all_to_all | solution.py:68
  79.1 6.6 %copy-start = (bf16[2,16,8192]{2,1,0:T(8,128)(2,1)S(1)}, bf16[2,16,8192]{2,1,0:T(8,128)(2,1)}, u32[]{:S(2)}) copy-start(bf16[2,16,8192]{2,1,0:T(8,128)(2,1)} %param.11) | copy-start | bytes 1572868
  86.0 10.4 %copy-start.3 = (f32[16,32]{1,0:T(8,128)S(1)}, f32[16,32]{1,0:T(8,128)}, u32[]{:S(2)}) copy-start(f32[16,32]{1,0:T(8,128)} %param.12) | copy-start | bytes 6148
  86.0 4.5 %collective-permute-start = (f32[16,32]{1,0:T(8,128)S(1)}, f32[16,32]{1,0:T(8,128)S(1)}, u32[]{:S(2)}, u32[]{:S(2)}) collective-permute-start(f32[16,32]{1,0:T(8,128)S(1)} %bitcast.89), channel_id=1, source_target_pairs={{0,1},{1,0},{2,3},{3,2},{4,5},{5,4},{6,7},{7,6},{8,9},{9,8},{10,11... | collective-permute-start | bytes 6152 | tf_op jit(solution)/shard_map/ppermute | solution.py:14
  90.6 5.9 %collective-permute-start.1 = (f32[16,32]{1,0:T(8,128)S(1)}, f32[16,32]{1,0:T(8,128)S(1)}, u32[]{:S(2)}, u32[]{:S(2)}) collective-permute-start(f32[16,32]{1,0:T(8,128)S(1)} %bitcast_add_fusion), channel_id=1, source_target_pairs={{0,2},{1,3},{2,0},{3,1},{4,6},{5,7},{6,4},{7,5},{8,10},{9,11},{10,... | collective-permute-start | bytes 6152 | tf_op jit(solution)/shard_map/ppermute | solution.py:14
